TPU v7x, 128 devices: a whole 4x4x4 slice. The times are simulated.
128 devices in a mesh: gx: 16 (over x, y), gy: 8 (over z, core).
Axes of the slice: x: 4, y: 4, z: 4, core: 2. Of those that a mesh axis runs over, the one named last changes fastest.
Arguments:
- level_set: float32 [16384, 8192], P('gx', 'gy'), may hold values from -6 to 6
- fuel_class: int32 [16384, 8192], P('gx', 'gy'), may hold values from 0 to 12
- ignition: int32 [2048, 1024], P('gx', 'gy'), may hold values 0 or 1
- counts: int32 [64, 32], P('gx', 'gy'), may hold values from 0 to 65536, as said below
- destination: int32 [64, 32], P('gx', 'gy'), may hold values from -1 to 15, as said below
- surface_wind: float32 [2, 2048, 1024], P(None, 'gx', 'gy'), may hold values from -9 to 9
- spread_table: float32 [13], replicated, may hold values from 0.03 to 0.25
- heat_table: float32 [13], replicated, may hold values from 1 to 8
- profile: float32 [4], replicated, may hold values from 0.2 to 1
Outputs:
- relocated: float32 [8, 256, 256, 256], P('gy', 'gx')
- heating: float32 [4, 2048, 1024], P(None, 'gx', 'gy')
Inputs may be any that keep to these rules, and one draw needn't show every extreme that they name: Zero marks a spare tile. In every row of devices along gx some device has all its tiles with counts > 0. -1 exactly where counts is 0. A tile goes to a device with the same gy index as its own. For each device there is an offset o such that its k-th burning tile (numbered in row-major order of its block) has destination (k + o) mod 16; so one device hands at most 1 tiles to one device.
All inputs are finite; a program needn't handle non-finite values. No bound on the sum of `ignition` on one device may be relied on, other than what follows from the above.
Results may differ from a plain program's by a relative error of at most 0.0003.
Values sent between devices are 32-bit elements; how exact they have to be, the bound alone decides.
A program may use at most 192 MiB of HBM per device.

v0:
```python
import jax
import jax.numpy as jnp
import numpy as np
from jax import lax
from jax.sharding import PartitionSpec as P

TILE = 256
REFINE = 8
NFUEL = 13


TIME_STEP = 0.6
IGNITE_DEPTH = 1.5
WIND_GAIN = 2.0
HIGHEST = lax.Precision.HIGHEST


def with_halo(cells, sides, width):
    for axis, dim in sides:
        count = lax.axis_size(axis)
        ends = count - 1
        head = lax.slice_in_dim(cells, 0, width, axis=dim)
        tail = lax.slice_in_dim(cells, cells.shape[dim] - width, cells.shape[dim], axis=dim)
        cells = jnp.concatenate(
            [
                lax.ppermute(tail, axis, [(i, (i + 1) % count) for i in range(ends)]),
                cells,
                lax.ppermute(head, axis, [((i + 1) % count, i) for i in range(ends)]),
            ],
            axis=dim,
        )
    return cells


def interp_table():
    coarse = TILE // REFINE
    interp = np.zeros((TILE + 4, coarse + 2), np.float32)
    for position in range(TILE + 4):
        centre = (position - 1.5) / REFINE + 0.5
        lower_cell = int(np.floor(centre))
        weight = centre - lower_cell
        interp[position, lower_cell] += 1.0 - weight
        interp[position, lower_cell + 1] += weight
    return interp


def mean_table():
    coarse = TILE // REFINE
    return np.kron(np.eye(coarse, dtype=np.float32), np.full((1, REFINE), 1.0 / REFINE, np.float32))


def advance(levels, spread, wind_x, wind_y):
    centre = levels[1:-1, 1:-1]
    back_x = centre - levels[:-2, 1:-1]
    ahead_x = levels[2:, 1:-1] - centre
    back_y = centre - levels[1:-1, :-2]
    ahead_y = levels[1:-1, 2:] - centre
    slope_x = 0.5 * (back_x + ahead_x)
    slope_y = 0.5 * (back_y + ahead_y)
    normal = jnp.sqrt(slope_x * slope_x + slope_y * slope_y + 1.0)
    tailwind = jnp.maximum((wind_x * slope_x + wind_y * slope_y) / normal, 0.0)
    spread_rate = spread * (1.0 + WIND_GAIN * tailwind * tailwind / (1.0 + tailwind * tailwind))
    upwind = jnp.sqrt(
        jnp.maximum(back_x, 0.0) ** 2
        + jnp.minimum(ahead_x, 0.0) ** 2
        + jnp.maximum(back_y, 0.0) ** 2
        + jnp.minimum(ahead_y, 0.0) ** 2
    )
    return centre - TIME_STEP * spread_rate * upwind


def burn_tile(extended, spread_ext, heat_tile, wind_tile):
    interp = jnp.asarray(interp_table(), jnp.float32)
    averaging = jnp.asarray(mean_table(), jnp.float32)

    def to_fire(field):
        inner_product = jnp.dot(
            interp, field, precision=HIGHEST, preferred_element_type=jnp.float32
        )
        return jnp.dot(
            inner_product, interp.T, precision=HIGHEST, preferred_element_type=jnp.float32
        )

    wind_x = to_fire(wind_tile[0])
    wind_y = to_fire(wind_tile[1])
    halfway = advance(extended, spread_ext[1:-1, 1:-1], wind_x[1:-1, 1:-1], wind_y[1:-1, 1:-1])
    second = advance(halfway, spread_ext[2:-2, 2:-2], wind_x[2:-2, 2:-2], wind_y[2:-2, 2:-2])
    burned_before = jnp.clip(0.5 - extended[2:-2, 2:-2], 0.0, 1.0)
    burned_after = jnp.clip(0.5 - second, 0.0, 1.0)
    release = heat_tile * (burned_after - burned_before) / (2.0 * TIME_STEP)
    partial_mean = jnp.dot(
        averaging, release, precision=HIGHEST, preferred_element_type=jnp.float32
    )
    tile_flux = jnp.dot(
        partial_mean, averaging.T, precision=HIGHEST, preferred_element_type=jnp.float32
    )
    return (second, tile_flux)


def lookup(fuel_code, spread_table, heat_table):
    spread = jnp.zeros(fuel_code.shape, jnp.float32)
    heat_field = jnp.zeros(fuel_code.shape, jnp.float32)
    for category in range(NFUEL):
        matches = fuel_code == float(category + 1)
        spread = jnp.where(matches, spread_table[category], spread)
        heat_field = jnp.where(matches, heat_table[category], heat_field)
    return (spread, heat_field)


def body(
    level_set,
    fuel_class,
    ignition,
    counts,
    destination,
    surface_wind,
    spread_table,
    heat_table,
    profile,
):
    coarse = TILE // REFINE
    width_x, width_y = level_set.shape
    tiles_x, tiles_y = counts.shape
    tile_count = tiles_x * tiles_y
    columns = lax.axis_size("gx")
    capacity = (tile_count + columns - 1) // columns
    slot_total = columns * capacity
    ignite = (
        ignition.astype(jnp.float32)[:, None, :, None]
        * jnp.ones((1, REFINE, 1, REFINE), jnp.float32)
    ).reshape(width_x, width_y)
    ignited = level_set - IGNITE_DEPTH * ignite
    fuel_code = fuel_class.astype(jnp.float32) + 1.0
    padded = with_halo(jnp.stack([ignited, fuel_code]), (("gx", 1), ("gy", 2)), 2)
    wind_pad = with_halo(surface_wind, (("gx", 1), ("gy", 2)), 1)
    active = (counts > 0).reshape(-1)
    tile_rank = jnp.cumsum(active.astype(jnp.int32)) - 1
    target = destination.reshape(-1)
    slot_rank = tile_rank // columns
    slot_ids = jnp.arange(slot_total, dtype=jnp.int32)
    slot_dest = slot_ids // capacity
    slot_place = slot_ids % capacity
    matches = (
        active[None, :]
        & (target[None, :] == slot_dest[:, None])
        & (slot_rank[None, :] == slot_place[:, None])
    )
    chosen = jnp.sum(
        jnp.where(matches, jnp.arange(tile_count, dtype=jnp.int32)[None, :], 0), axis=1
    )
    filled = jnp.any(matches, axis=1)

    def extract(tile_index):
        block_x = tile_index // tiles_y
        block_y = tile_index % tiles_y
        extended = lax.dynamic_slice(
            padded, (jnp.int32(0), block_x * TILE, block_y * TILE), (2, TILE + 4, TILE + 4)
        )
        wind_tile = lax.dynamic_slice(
            wind_pad,
            (jnp.int32(0), block_x * coarse, block_y * coarse),
            (2, coarse + 2, coarse + 2),
        )
        return (extended, wind_tile)

    def nothing():
        return (jnp.zeros((TILE, TILE), jnp.float32), jnp.zeros((coarse, coarse), jnp.float32))

    def burn_coded(levels, codes, wind_tile):
        spread_ext, heat_ext = lookup(codes, spread_table, heat_table)
        return burn_tile(levels, spread_ext, heat_ext[2:-2, 2:-2], wind_tile)

    def run_tile(tile_index):
        extended, wind_tile = extract(tile_index)

        def compute():
            return burn_coded(extended[0], extended[1], wind_tile)

        return lax.cond(active[tile_index], compute, nothing)

    updated, fluxes = lax.map(run_tile, jnp.arange(tile_count, dtype=jnp.int32))
    outgoing = jnp.where(filled[:, None, None], jnp.take(updated, chosen, axis=0), 0.0)
    outgoing = outgoing.reshape(columns, capacity, TILE, TILE)
    incoming = lax.all_to_all(outgoing, "gx", split_axis=0, concat_axis=0, tiled=True)
    relocated = incoming.reshape(1, slot_total, TILE, TILE)
    fluxes = jnp.where(active[:, None, None], fluxes, 0.0)
    flux_grid = (
        fluxes.reshape(tiles_x, tiles_y, coarse, coarse)
        .transpose(0, 2, 1, 3)
        .reshape(tiles_x * coarse, tiles_y * coarse)
    )
    heating = profile[:, None, None] * flux_grid[None]
    return (relocated, heating)


def solution(mesh):
    in_specs = (
        P("gx", "gy"),
        P("gx", "gy"),
        P("gx", "gy"),
        P("gx", "gy"),
        P("gx", "gy"),
        P(None, "gx", "gy"),
        P(),
        P(),
        P(),
    )
    out_specs = (P("gy", "gx", None, None), P(None, "gx", "gy"))
    return jax.shard_map(body, mesh=mesh, in_specs=in_specs, out_specs=out_specs, check_vma=False)
```

profile of v0, /device:TPU:80, one launch (start us, length us, event | category | flops | bytes accessed | tf_op | source)
XLA Modules:
  0.0 768.4 jit_solution(6172352510239253165)
XLA Ops:
  1.5 21.4 %mul.247 = f32[128,8,128,8]{3,2,1,0:T(8,128)} broadcast(f32[128,128]{1,0:T(8,128)S(1)} %convert_multiply_fusion), dimensions={0,2} | broadcast | bytes 4259840 | tf_op jit(solution)/shard_map/mul | solution.py:129
  22.9 48.3 %mul.248 = f32[1024,1024]{1,0:T(8,128)} reshape(f32[128,8,128,8]{3,2,1,0:T(8,128)} %mul.247) | data formatting | bytes 8388608 | tf_op jit(solution)/shard_map/mul | solution.py:132
  71.3 6.2 add_bitcast_fusion
  77.5 3.3 collective-permute-start
  80.8 2.7 collective-permute-start.1
  83.5 3.2 collective-permute-start.4
  86.7 2.7 collective-permute-start.5
  89.4 4.1 pad_maximum_fusion
  94.3 1.9 collective-permute-start.6
  96.2 3.6 collective-permute-start.7
  99.9 24.1 %concatenate.12 = f32[2,1028,1024]{2,1,0:T(8,128)} concatenate(f32[2,2,1024]{2,1,0:T(2,128)S(1)} %collective-permute-done, f32[2,1024,1024]{2,1,0:T(8,128)} %pad_maximum_fusion, f32[2,2,1024]{2,1,0:T(2,128)S(1)} %collective-permute-done.1), dimensions={1} | concatenate | bytes 16842752 | tf_op jit(solution)/shard_map/concatenate | solution.py:24
  124.0 1.9 fusion.49
  126.2 1.9 collective-permute-start.2
  128.5 3.8 collective-permute-start.3
  134.0 11.5 %concatenate.13 = f32[2,1028,1028]{2,1,0:T(8,128)} concatenate(f32[2,1028,2]{2,1,0:T(8,128)S(1)} %copy.26, f32[2,1028,1024]{2,1,0:T(8,128)} %concatenate.12, f32[2,1028,2]{2,1,0:T(8,128)S(1)} %copy.27), dimensions={2} | concatenate | bytes 16908544 | tf_op jit(solution)/shard_map/concatenate | solution.py:24
  145.6 114.0 %while.16 = (s32[]{:T(128)}, f32[16,256,256]{2,1,0:T(8,128)}, f32[16,32,32]{2,1,0:T(8,128)S(1)}, s32[16]{0:T(128)S(1)}, pred[16]{0:T(512)(128)(4,1)S(1)}, /*inde...) while((s32[]{:T(128)}, f32[16,256,256]{2,1,0:T(8,128)}, ...), condition=%wide.region_6.7_spmd.clone.clone, body=%wide.region_3.6_spmd.sunk.clone.sunk.clone | while | flops 98801584 | bytes 10682152 | solution.py:181
  151.0 1.7 constant_dynamic-update-slice_fusion.6
  158.1 1.7 constant_dynamic-update-slice_fusion.6
  165.3 1.7 constant_dynamic-update-slice_fusion.6
  259.6 5.0 gather_fusion
  264.5 4.8 fusion.38
  269.4 425.3 %all-to-all-start = ((f32[16,1,256,256]{3,2,1,0:T(8,128)}), f32[16,1,256,256]{3,2,1,0:T(8,128)}, u32[]{:S(2)}, u32[]{:S(2)}) async-start(f32[16,1,256,256]{3,2,1,0:T(8,128)} %fusion.38), calls=%async_computation | async-start | bytes 8388608 | tf_op jit(solution)/shard_map/all_to_all | solution.py:184
  695.9 67.9 %all-to-all-done = f32[16,1,256,256]{3,2,1,0:T(8,128)} async-done(((f32[16,1,256,256]{3,2,1,0:T(8,128)}), f32[16,1,256,256]{3,2,1,0:T(8,128)}, u32[]{:S(2)}, u32[]{:S(2)}) %all-to-all-start) | async-done | bytes 4194336 | tf_op jit(solution)/shard_map/all_to_all | solution.py:184
  763.8 4.6 copy.46
  (158 shorter events, 69.2 us)
Async XLA Ops:
  77.4 6.0 copy-start.4
  77.5 22.4 %collective-permute-start = (f32[2,2,1024]{2,1,0:T(2,128)S(1)}, f32[2,2,1024]{2,1,0:T(2,128)S(1)}, u32[]{:S(2)}, u32[]{:S(2)}) collective-permute-start(f32[2,2,1024]{2,1,0:T(2,128)S(1)} %get-tuple-element.542), channel_id=1, source_target_pairs={{0,8},{8,16},{16,24},{24,32},{32,40},{40,48},{48,56},{56,64},{64,7... | collective-permute-start | bytes 49160 | tf_op jit(solution)/shard_map/ppermute | solution.py:26
  80.8 19.1 %collective-permute-start.1 = (f32[2,2,1024]{2,1,0:T(2,128)S(1)}, f32[2,2,1024]{2,1,0:T(2,128)S(1)}, u32[]{:S(2)}, u32[]{:S(2)}) collective-permute-start(f32[2,2,1024]{2,1,0:T(2,128)S(1)} %get-tuple-element.541), channel_id=1, source_target_pairs={{8,0},{16,8},{24,16},{32,24},{40,32},{48,40},{56,48},{64,56},{72,6... | collective-permute-start | bytes 49160 | tf_op jit(solution)/shard_map/ppermute | solution.py:28
  83.5 10.7 %collective-permute-start.4 = (f32[2,1,128]{2,1,0:T(1,128)S(1)}, f32[2,1,128]{2,1,0:T(1,128)S(1)}, u32[]{:S(2)}, u32[]{:S(2)}) collective-permute-start(f32[2,1,128]{2,1,0:T(1,128)S(1)} %get-tuple-element.545), channel_id=1, source_target_pairs={{0,8},{8,16},{16,24},{24,32},{32,40},{40,48},{48,56},{56,64},{64,7... | collective-permute-start | bytes 3080 | tf_op jit(solution)/shard_map/ppermute | solution.py:26
  86.7 6.8 copy-start.6
  86.7 7.1 copy-start.5
  86.7 7.5 collective-permute-start.5
  94.3 38.1 %collective-permute-start.6 = (f32[2,130,1]{2,1,0:T(8,128)S(1)}, f32[2,130,1]{2,1,0:T(8,128)S(1)}, u32[]{:S(2)}, u32[]{:S(2)}) collective-permute-start(f32[2,130,1]{2,1,0:T(8,128)S(1)} %get-tuple-element.543), channel_id=1, source_target_pairs={{0,1},{1,2},{2,3},{3,4},{4,5},{5,6},{6,7},{8,9},{9,10},{10,11},{11... | collective-permute-start | bytes 3128 | tf_op jit(solution)/shard_map/ppermute | solution.py:26
  96.2 36.1 %collective-permute-start.7 = (f32[2,130,1]{2,1,0:T(8,128)S(1)}, f32[2,130,1]{2,1,0:T(8,128)S(1)}, u32[]{:S(2)}, u32[]{:S(2)}) collective-permute-start(f32[2,130,1]{2,1,0:T(8,128)S(1)} %get-tuple-element.544), channel_id=1, source_target_pairs={{1,0},{2,1},{3,2},{4,3},{5,4},{6,5},{7,6},{9,8},{10,9},{11,10},{12... | collective-permute-start | bytes 3128 | tf_op jit(solution)/shard_map/ppermute | solution.py:28
  126.2 6.3 collective-permute-start.2
  128.5 5.1 collective-permute-start.3
  134.0 11.5 %copy-start.2 = (f32[13]{0:T(128)S(1)}, f32[13]{0:T(128)}, u32[]{:S(2)}) copy-start(f32[13]{0:T(128)} %param.21) | copy-start | bytes 160
  134.0 11.5 %copy-start.3 = (f32[13]{0:T(128)S(1)}, f32[13]{0:T(128)}, u32[]{:S(2)}) copy-start(f32[13]{0:T(128)} %param.22) | copy-start | bytes 160
  269.4 425.7 %copy-start.7 = (f32[4]{0:T(128)S(1)}, f32[4]{0:T(128)}, u32[]{:S(2)}) copy-start(f32[4]{0:T(128)} %param.23) | copy-start | bytes 52
  269.4 494.4 %all-to-all-start = ((f32[16,1,256,256]{3,2,1,0:T(8,128)}), f32[16,1,256,256]{3,2,1,0:T(8,128)}, u32[]{:S(2)}, u32[]{:S(2)}) async-start(f32[16,1,256,256]{3,2,1,0:T(8,128)} %fusion.38), calls=%async_computation | async-start | bytes 8388608 | tf_op jit(solution)/shard_map/all_to_all | solution.py:184
where the time goes:
time: 775 us; the launch traced here: 768 us
  starting transfers between devices  448 us (58%)
  local copies, waits for them, and re-layouts  176 us (23%)
  waiting for transfers between devices  68.6 us (9%)
  loops' own time  56.8 us (7%)
  other arithmetic  17.5 us (2%)
    all_to_all x1, starting transfers between devices, body(): lax.all_to_all(outgoing, 'gx', split_axis=0, concat_axis=0, tiled=True)  425 us
    all_to_all x1, waiting for transfers between devices, body(): lax.all_to_all(outgoing, 'gx', split_axis=0, concat_axis=0, tiled=True)  67.9 us
    another operation x1, loops' own time, body(): updated, fluxes = lax.map(run_tile, jnp.arange(tile_count, dtype=jnp.int32))  56.6 us
    mul x1, local copies, waits for them, and re-layouts, body(): ignited = level_set - IGNITE_DEPTH * ignite  48.3 us
    concatenate x2, local copies, waits for them, and re-layouts, with_halo(): jnp.concatenate([lax.ppermute(tail, axis, [(i, (i + 1) % count) for i in...  35.6 us
    dynamic_update_slice x32, local copies, waits for them, and re-layouts, body(): updated, fluxes = lax.map(run_tile, jnp.arange(tile_count, dtype=jnp.int32))  26.7 us
    mul x1, local copies, waits for them, and re-layouts, body(): ignition.astype(jnp.float32)[:, None, :, None]  21.4 us
  transfers between devices with their start and end apart: 9, of which 2 were waited for; matrix products, arithmetic and copies ran while one was open for 4% of the time, Pallas kernels for 0%

commit v1 on v0

v1 whole, which is shorter than its diff:
```python
import jax
import jax.numpy as jnp
from jax import lax
from jax.experimental import pallas as pl
from jax.experimental.pallas import tpu as pltpu
from jax.sharding import PartitionSpec as P

TILE = 256
REFINE = 8
NFUEL = 13
LEV = 4
TIME_STEP = 0.6
IGNITE_DEPTH = 1.5
N_GX = 16
N_GY = 8
SIDE = 1024
COARSE = 128
RING = 384
TINY = 1e-30
MESH = pl.DeviceIdType.MESH
F32 = jnp.float32
BF16 = jnp.bfloat16

OFFSETS = (
    (2, 2), (2, 1), (1, 2), (2, 3), (3, 2), (1, 1), (3, 3), (1, 3),
    (3, 1), (2, 0), (0, 2), (1, 0), (0, 1), (3, 0), (0, 3), (0, 0),
)


def split(x):
    high = x.astype(BF16)
    return high, (x - high.astype(F32)).astype(BF16)


def dot2(a, b):
    high, low = split(a)
    return jnp.dot(high, b, preferred_element_type=F32) + jnp.dot(
        low, b, preferred_element_type=F32
    )


def advance(centre, up, down, left, right, wind_x, wind_y, reach):
    back_x = centre - up
    ahead_x = down - centre
    back_y = centre - left
    ahead_y = right - centre
    twice_x = down - up
    twice_y = right - left
    push = jnp.maximum(wind_x * twice_x + wind_y * twice_y, 0.0)
    push2 = push * push
    whole = twice_x * twice_x + twice_y * twice_y + 4.0 + push2
    gain = whole + 2.0 * push2
    px = jnp.maximum(back_x, 0.0)
    nx = jnp.minimum(ahead_x, 0.0)
    py = jnp.maximum(back_y, 0.0)
    ny = jnp.minimum(ahead_y, 0.0)
    upwind2 = (px * px + nx * nx) + (py * py + ny * ny)
    scale = lax.rsqrt(jnp.maximum(upwind2, TINY) * (whole * whole))
    return centre - (reach * gain) * (upwind2 * scale)


def lookup(table, scale, codes):
    values = [table[t] * scale for t in range(NFUEL)]
    bit = 1
    while len(values) > 1:
        odd = (codes & bit) != 0
        values = [
            jnp.where(odd, values[t + 1], values[t]) if t + 1 < len(values) else values[t]
            for t in range(0, len(values), 2)
        ]
        bit *= 2
    return values[0]


def kernel(
    level_hbm, fuel_hbm, ignition_hbm, wind_hbm, spread_hbm, heat_hbm, plan_hbm, profile_hbm,
    out, heating,
    levels, spreads, fuels, winds, level, spread, heat, halfway, fire_wind,
    ignition, wind, spread_table, heat_table, plan, profile,
    wind_pad, row_weight, ignite, stage, release, flux,
    row_send, row_recv, col_send, col_recv, diag_send, diag_recv,
    small_sem, level_sem, fuel_sem,
    row_sem, col_sem, diag_sem, row_rsem, col_rsem, diag_rsem, send_sem, recv_sem, own_sem,
):
    gx = lax.axis_index("gx")
    gy = lax.axis_index("gy")
    my_x = gx // 4
    my_y = gx % 4
    gx_at = ((gx + N_GX - 1) % N_GX, (gx + 1) % N_GX)
    gy_at = ((gy + N_GY - 1) % N_GY, (gy + 1) % N_GY)

    small = [
        pltpu.make_async_copy(source, here, small_sem.at[n])
        for n, (source, here) in enumerate((
            (ignition_hbm, ignition), (spread_hbm, spread_table), (wind_hbm, wind),
            (heat_hbm, heat_table), (plan_hbm, plan), (profile_hbm, profile),
        ))
    ]
    for copy in small:
        copy.start()
    loads = []
    for k in range(16):
        block = (pl.ds(k // 4 * TILE, TILE), pl.ds(k % 4 * TILE, TILE))
        loads.append(
            pltpu.make_async_copy(
                level_hbm.at[block], levels.at[k, pl.ds(8, TILE), pl.ds(0, TILE)], level_sem.at[k]
            )
        )
        loads.append(pltpu.make_async_copy(fuel_hbm.at[block], fuels.at[k], fuel_sem.at[k]))
    for copy in loads:
        copy.start()

    barrier = pltpu.get_barrier_semaphore()
    for ox, oy in OFFSETS[:-1]:
        peer = ((my_x + ox) % 4) * 4 + (my_y + oy) % 4
        pl.semaphore_signal(
            barrier, inc=1, device_id={"gx": peer, "gy": gy}, device_id_type=MESH
        )
    for b in range(2):
        for px in (gx, gx_at[0], gx_at[1]):
            pl.semaphore_signal(
                barrier, inc=1, device_id={"gx": px, "gy": gy_at[b]}, device_id_type=MESH
            )

    lane = lax.broadcasted_iota(jnp.int32, (1, 128), 1)
    low_lane = lane < 64

    levels[16] = jnp.zeros((TILE + 16, RING), F32)
    spreads[16] = jnp.zeros((TILE + 16, RING), F32)
    fuels[16] = jnp.zeros((TILE, TILE), jnp.int32)
    winds[16] = jnp.zeros((96, 2 * RING), BF16)
    flux[16] = jnp.zeros((32, 128), F32)

    fire_row = (lax.broadcasted_iota(jnp.int32, (TILE + 16, 96), 0) - 8).astype(F32)
    coarse_row = lax.broadcasted_iota(jnp.int32, (TILE + 16, 96), 1)
    coarse_row = (jnp.where(coarse_row >= 48, coarse_row - 48, coarse_row) - 8).astype(F32)
    tent = 1.0 - jnp.abs((fire_row + 0.5) * (1.0 / REFINE) - 0.5 - coarse_row)
    row_weight[...] = jnp.maximum(tent, 0.0).astype(BF16)

    for copy in small:
        copy.wait()
    cell = lax.broadcasted_iota(jnp.int32, (COARSE, TILE), 0)
    at = lax.broadcasted_iota(jnp.int32, (COARSE, TILE), 1) // REFINE
    burning = ignition[...].astype(F32).astype(BF16)
    for t in range(4):
        repeat = jnp.where(cell == at + t * 32, IGNITE_DEPTH, 0.0).astype(BF16)
        ignite[t] = jnp.dot(burning, repeat, preferred_element_type=F32)

    def prepare(tile_x, tile_y, block, subs, halves):
        k = tile_x * 4 + tile_y
        for half in halves:
            lanes = pl.ds(half * 128, 128)
            burned = ignite[tile_y, pl.ds(pl.multiple_of(tile_x * 32 + block * 8, 8), 8), lanes]
            for s in subs:
                inner = pl.ds(pl.multiple_of(block * 64 + s * 8 + 8, 8), 8)
                levels[k, inner, lanes] = levels[k, inner, lanes] - burned[s : s + 1, :]
                codes = fuels[k, pl.ds(pl.multiple_of(block * 64 + s * 8, 8), 8), lanes]
                spreads[k, inner, lanes] = lookup(spread_table, TIME_STEP, codes)

    for copy in loads:
        copy.wait()

    def prepare_edges(block, carry):
        prepare(block // 4, 0, block % 4, range(8), (0,))
        prepare(block // 4, 3, block % 4, range(8), (1,))
        return carry

    lax.fori_loop(0, 16, prepare_edges, 0)
    for tile_y, halves in ((0, (1,)), (1, (0, 1)), (2, (0, 1)), (3, (0,))):
        prepare(0, tile_y, 0, (0,), halves)
        prepare(3, tile_y, 3, (7,), halves)

    wind_edges = (0, COARSE - 8)
    for b in range(2):
        rows = pl.ds(b * (TILE - 8) + 8, 8)
        for t in range(4):
            lanes = pl.ds(t * TILE, TILE)
            row_send[b, 0:8, lanes] = levels[b * 12 + t, rows, 0:TILE]
            row_send[b, 8:16, lanes] = spreads[b * 12 + t, rows, 0:TILE]
        for c in range(2):
            row_send[b, c * 8 : c * 8 + 8, SIDE : SIDE + 128] = wind[c, pl.ds(wind_edges[b], 8), :]
        for a in range(2):
            diag_send[b * 2 + a, 0:8, :] = levels[b * 12 + a * 3, rows, pl.ds(a * 128, 128)]
            for c in range(2):
                diag_send[b * 2 + a, 8 + c * 8 : 16 + c * 8, :] = wind[c, pl.ds(wind_edges[b], 8), :]
    for a in range(2):
        source = pl.ds(a * 128, 128)
        packed = jnp.zeros((32, 128), F32)
        for g in range(32):
            k = g // 8 * 4 + a * 3
            rows = pl.ds(8 + g % 8 * 32, 32)
            to_level = (4 * g + 2 - (126 if a else 0)) % 128
            to_spread = (4 * g + 1 - (127 if a else 0)) % 128
            moved = jnp.where(
                lane % 4 == 1,
                pltpu.roll(spreads[k, rows, source], to_spread, 1),
                pltpu.roll(levels[k, rows, source], to_level, 1),
            )
            if g < 8:
                to_wind = (4 * g - (127 if a else 0)) % 128
                moved = jnp.where(
                    lane % 4 == 0,
                    pltpu.roll(wind[g // 4, pl.ds((g % 4) * 32, 32), :], to_wind, 1),
                    moved,
                )
            packed = jnp.where(lane // 4 == g, moved, packed)
        col_send[a] = packed

    pl.semaphore_wait(barrier, len(OFFSETS) - 1 + 6)

    halos = []
    for b in range(2):
        halos.append(
            pltpu.make_async_remote_copy(
                src_ref=row_send.at[b], dst_ref=row_recv.at[1 - b],
                send_sem=row_sem.at[b], recv_sem=row_rsem.at[1 - b],
                device_id={"gx": gx_at[b], "gy": gy}, device_id_type=MESH,
            )
        )
        halos.append(
            pltpu.make_async_remote_copy(
                src_ref=col_send.at[b], dst_ref=col_recv.at[1 - b],
                send_sem=col_sem.at[b], recv_sem=col_rsem.at[1 - b],
                device_id={"gx": gx, "gy": gy_at[b]}, device_id_type=MESH,
            )
        )
        for a in range(2):
            k = b * 2 + a
            halos.append(
                pltpu.make_async_remote_copy(
                    src_ref=diag_send.at[k], dst_ref=diag_recv.at[3 - k],
                    send_sem=diag_sem.at[k], recv_sem=diag_rsem.at[3 - k],
                    device_id={"gx": gx_at[b], "gy": gy_at[a]}, device_id_type=MESH,
                )
            )
    for copy in halos:
        copy.start()

    def prepare_rest(block, carry):
        for tile_y, halves in ((0, (1,)), (1, (0, 1)), (2, (0, 1)), (3, (0,))):
            prepare(block // 4, tile_y, block % 4, range(8), halves)
        return carry

    for tile_y, halves in ((0, (1,)), (1, (0, 1)), (2, (0, 1)), (3, (0,))):
        prepare(0, tile_y, 0, range(1, 8), halves)
        prepare(3, tile_y, 3, range(7), halves)
    lax.fori_loop(1, 15, prepare_rest, 0)

    edge_lanes = pl.ds(TILE, 128)

    def set_edges(block, carry):
        rows = pl.ds(pl.multiple_of(block % 4 * 64 + 8, 8), 64)
        k = block // 4 * 4
        for ref in (levels, spreads):
            ref[k, rows, edge_lanes] = ref[k + 1, rows, 0:128]
            for t in (1, 2):
                ref[k + t, rows, edge_lanes] = jnp.where(
                    low_lane, ref[k + t + 1, rows, 0:128], ref[k + t - 1, rows, 128:256]
                )
            ref[k + 3, rows, edge_lanes] = ref[k + 2, rows, 128:256]
        return carry

    lax.fori_loop(0, 16, set_edges, 0)

    for c in range(2):
        wind_pad[c, 8 : 8 + COARSE, 0:128] = wind[c]

    column = lax.broadcasted_iota(jnp.int32, (256, RING), 0)
    column = jnp.where(column >= 192, column - 256, column)
    fire = lax.broadcasted_iota(jnp.int32, (256, RING), 1)
    fire = jnp.where(fire >= 320, fire - RING, fire)
    offset = (fire.astype(F32) + 0.5) * (1.0 / REFINE) - 0.5 - column.astype(F32)

    has_row = (gx > 0, gx < N_GX - 1)
    has_col = (gy > 0, gy < N_GY - 1)

    for copy in halos:
        copy.wait()

    cols = [jnp.where(has_col[a], col_recv[a], 0.0) for a in range(2)]
    for g in range(32):
        rows = pl.ds(8 + g % 8 * 32, 32)
        for ref, item, last in ((levels, 2, 126), (spreads, 1, 127)):
            k = g // 8 * 4
            got = pltpu.roll(cols[0], (last - (4 * g + item)) % 128, 1)
            ref[k, rows, edge_lanes] = jnp.where(low_lane, ref[k, rows, edge_lanes], got)
            got = pltpu.roll(cols[1], (0 - (4 * g + item)) % 128, 1)
            ref[k + 3, rows, edge_lanes] = jnp.where(low_lane, got, ref[k + 3, rows, edge_lanes])
        if g < 8:
            ends = [pltpu.roll(cols[a], ((0 if a else 127) - 4 * g) % 128, 1) for a in range(2)]
            wind_pad[g // 4, pl.ds(8 + (g % 4) * 32, 32), 128:256] = jnp.where(
                low_lane, ends[1], ends[0]
            )
    for b in range(2):
        rows = pl.ds(b * (TILE + 8), 8)
        from_rows = pl.ds(8 if b else TILE, 8)
        for k in range(16):
            if k // 4 == b * 3:
                t = k % 4
                for ref, part in ((levels, 0), (spreads, 8)):
                    got = row_recv[b, part : part + 8, :]
                    ref[k, rows, 0:TILE] = jnp.where(has_row[b], got[:, t * TILE : t * TILE + TILE], 0.0)
                    corner = [
                        jnp.where(has_col[a], diag_recv[b * 2 + a, 0:8, :], 0.0) for a in range(2)
                    ]
                    last = corner[0] if t == 0 else got[:, t * TILE - 128 : t * TILE]
                    after = corner[1] if t == 3 else got[:, t * TILE + TILE : t * TILE + TILE + 128]
                    ref[k, rows, edge_lanes] = jnp.where(
                        has_row[b], jnp.where(low_lane, after, last), 0.0
                    )
            else:
                for ref in (levels, spreads):
                    ref[k, rows, :] = ref[k + (4 if b else -4), from_rows, :]
        wind_at = pl.ds(b * (COARSE + 8), 8)
        for c in range(2):
            wind_pad[c, wind_at, 0:128] = jnp.where(
                has_row[b], row_recv[b, c * 8 : c * 8 + 8, SIDE : SIDE + 128], 0.0
            )
            ends = [
                jnp.where(has_col[a], diag_recv[b * 2 + a, 8 + c * 8 : 16 + c * 8, :], 0.0)
                for a in range(2)
            ]
            wind_pad[c, wind_at, 128:256] = jnp.where(
                has_row[b], jnp.where(low_lane, ends[1], ends[0]), 0.0
            )

    for t in range(4):
        weight = jnp.maximum(1.0 - jnp.abs(offset + 32.0 * t), 0.0).astype(BF16)
        for c in range(2):
            high, low = split(dot2(wind_pad[c], weight))
            for tx in range(4):
                lanes = pl.ds(c * RING, RING)
                winds[tx * 4 + t, 0:48, lanes] = high[tx * 32 : tx * 32 + 48]
                winds[tx * 4 + t, 48:96, lanes] = low[tx * 32 : tx * 32 + 48]

    sub = lax.broadcasted_iota(jnp.int32, (8, RING), 0)
    sub_in = lax.broadcasted_iota(jnp.int32, (8, TILE), 0)
    place = jnp.where(
        lax.broadcasted_iota(jnp.int32, (TILE, 128), 0) // REFINE
        == lax.broadcasted_iota(jnp.int32, (TILE, 128), 1),
        1.0,
        0.0,
    ).astype(BF16)

    def eight(i):
        return pl.ds(pl.multiple_of(i * 8, 8), 8)

    def one_tile(j, carry):
        ox = jnp.int32(0)
        oy = jnp.int32(0)
        for i, (dx, dy) in enumerate(OFFSETS):
            now = (j == i).astype(jnp.int32)
            ox = ox + now * dx
            oy = oy + now * dy
        target = ((my_x + ox) % 4) * 4 + (my_y + oy) % 4

        chosen = plan[target]
        level[0 : TILE + 16, :] = levels[chosen]
        spread[...] = spreads[chosen]
        heat[...] = lookup(heat_table, 1.0 / (2.0 * TIME_STEP * REFINE * REFINE), fuels[chosen])
        fire_wind[...] = jnp.dot(row_weight[...], winds[chosen], preferred_element_type=F32)

        def first(i, carry):
            above, centre = carry
            below = level[eight(i + 1), :]
            up = pltpu.roll(jnp.where(sub == 7, above, centre), 1, 0)
            down = pltpu.roll(jnp.where(sub == 0, below, centre), 7, 0)
            left = pltpu.roll(centre, 1, 1)
            right = pltpu.roll(centre, RING - 1, 1)
            halfway[eight(i), :] = advance(
                centre, up, down, left, right,
                fire_wind[eight(i), 0:RING], fire_wind[eight(i), RING : 2 * RING],
                spread[eight(i), :],
            )
            return centre, below

        level[TILE + 16 :, :] = level[TILE + 8 : TILE + 16, :]
        lax.fori_loop(0, TILE // 8 + 2, first, (level[0:8, :], level[0:8, :]), unroll=2)

        def second(i, carry):
            above, centre = carry
            below = halfway[eight(i + 2), :]
            inner = centre[:, 0:TILE]
            up = pltpu.roll(jnp.where(sub_in == 7, above[:, 0:TILE], inner), 1, 0)
            down = pltpu.roll(jnp.where(sub_in == 0, below[:, 0:TILE], inner), 7, 0)
            left = pltpu.roll(centre, 1, 1)[:, 0:TILE]
            right = pltpu.roll(centre, RING - 1, 1)[:, 0:TILE]
            result = advance(
                inner, up, down, left, right,
                fire_wind[eight(i + 1), 0:TILE], fire_wind[eight(i + 1), RING : RING + TILE],
                spread[eight(i + 1), 0:TILE],
            )
            before = jnp.clip(0.5 - level[eight(i + 1), 0:TILE], 0.0, 1.0)
            after = jnp.clip(0.5 - result, 0.0, 1.0)
            released = heat[eight(i), :] * (after - before)
            release[0, eight(i), :] = released[:, 0:128]
            release[1, eight(i), :] = released[:, 128:256]
            stage[target, eight(i), :] = result
            return centre, below

        lax.fori_loop(0, TILE // 8, second, (halfway[0:8, :], halfway[8:16, :]), unroll=2)

        @pl.when(j < len(OFFSETS) - 1)
        def _():
            pltpu.make_async_remote_copy(
                src_ref=stage.at[target], dst_ref=out.at[gx],
                send_sem=send_sem.at[j], recv_sem=recv_sem.at[j],
                device_id={"gx": target, "gy": gy}, device_id_type=MESH,
            ).start()

        rows = []
        for half in range(2):
            total = release[half, pl.ds(0, 32, stride=8), :]
            for s in range(1, 8):
                total = total + release[half, pl.ds(s, 32, stride=8), :]
            rows.append(total)
        flux[target] = dot2(jnp.concatenate(rows, axis=1), place)
        return carry

    lax.fori_loop(0, len(OFFSETS), one_tile, 0)

    own = pltpu.make_async_copy(stage.at[gx], out.at[gx], own_sem)
    own.start()

    for tx in range(4):
        band = jnp.zeros((32, 128), F32)
        for ty in range(4):
            band = band + pltpu.roll(flux[plan[16 + tx * 4 + ty]], ty * 32, 1)
        for l in range(LEV):
            heating[l, tx * 32 : tx * 32 + 32, :] = profile[l] * band

    own.wait()

    def finish(j, carry):
        pltpu.make_async_remote_copy(
            src_ref=stage.at[gx], dst_ref=out.at[gx],
            send_sem=send_sem.at[j], recv_sem=recv_sem.at[j],
            device_id={"gx": (gx + 1) % N_GX, "gy": gy}, device_id_type=MESH,
        ).wait()
        return carry

    lax.fori_loop(0, len(OFFSETS) - 1, finish, 0)


def body(
    level_set, fuel_class, ignition, counts, destination, surface_wind, spread_table, heat_table, profile
):
    hbm = pl.BlockSpec(memory_space=pltpu.HBM)
    vmem = pl.BlockSpec(memory_space=pltpu.VMEM)
    dma = pltpu.SemaphoreType.DMA

    target = jnp.where(counts > 0, destination, 16).reshape(16)
    ids = jnp.arange(16, dtype=jnp.int32)
    taken = jnp.min(jnp.where(target[None, :] == ids[:, None], ids[None, :], 16), axis=1)
    plan = jnp.concatenate([taken, target])

    relocated, heating = pl.pallas_call(
        kernel,
        out_shape=(
            jax.ShapeDtypeStruct((N_GX, TILE, TILE), F32),
            jax.ShapeDtypeStruct((LEV, COARSE, COARSE), F32),
        ),
        in_specs=[hbm] * 8,
        out_specs=(vmem, vmem),
        scratch_shapes=[
            pltpu.VMEM((17, TILE + 16, RING), F32),
            pltpu.VMEM((17, TILE + 16, RING), F32),
            pltpu.VMEM((17, TILE, TILE), jnp.int32),
            pltpu.VMEM((17, 96, 2 * RING), BF16),
            pltpu.VMEM((TILE + 24, RING), F32),
            pltpu.VMEM((TILE + 16, RING), F32),
            pltpu.VMEM((TILE, TILE), F32),
            pltpu.VMEM((TILE + 16, RING), F32),
            pltpu.VMEM((TILE + 16, 2 * RING), F32),
            pltpu.VMEM((COARSE, COARSE), jnp.int32),
            pltpu.VMEM((2, COARSE, COARSE), F32),
            pltpu.SMEM((NFUEL,), F32),
            pltpu.SMEM((NFUEL,), F32),
            pltpu.SMEM((32,), jnp.int32),
            pltpu.SMEM((LEV,), F32),
            pltpu.VMEM((2, COARSE + 16, 256), F32),
            pltpu.VMEM((TILE + 16, 96), BF16),
            pltpu.VMEM((4, COARSE, TILE), F32),
            pltpu.VMEM((N_GX, TILE, TILE), F32),
            pltpu.VMEM((2, TILE, 128), F32),
            pltpu.VMEM((17, 32, 128), F32),
            pltpu.VMEM((2, 16, SIDE + 128), F32),
            pltpu.VMEM((2, 16, SIDE + 128), F32),
            pltpu.VMEM((2, 32, 128), F32),
            pltpu.VMEM((2, 32, 128), F32),
            pltpu.VMEM((4, 24, 128), F32),
            pltpu.VMEM((4, 24, 128), F32),
            dma((6,)),
            dma((16,)),
            dma((16,)),
            dma((2,)),
            dma((2,)),
            dma((4,)),
            dma((2,)),
            dma((2,)),
            dma((4,)),
            dma((16,)),
            dma((16,)),
            dma,
        ],
        compiler_params=pltpu.CompilerParams(
            collective_id=0, has_side_effects=True, vmem_limit_bytes=44 << 20
        ),
    )(
        level_set, fuel_class, ignition, surface_wind, spread_table, heat_table, plan, profile
    )
    return relocated.reshape(1, N_GX, TILE, TILE), heating


def solution(mesh):
    in_specs = (
        P("gx", "gy"),
        P("gx", "gy"),
        P("gx", "gy"),
        P("gx", "gy"),
        P("gx", "gy"),
        P(None, "gx", "gy"),
        P(),
        P(),
        P(),
    )
    out_specs = (P("gy", "gx", None, None), P(None, "gx", "gy"))
    return jax.shard_map(body, mesh=mesh, in_specs=in_specs, out_specs=out_specs, check_vma=False)
```

time: 775 us -> 94.2 us (0.12)
  the two profiles are of different devices: /device:TPU:80 before, /device:TPU:43 now
where the time goes in v1:
time: 94.2 us; the launch traced here: 93.9 us
  Pallas kernels  83.6 us (89%)
  local copies, waits for them, and re-layouts  8.7 us (9%)
    pallas_call x1, Pallas kernels, body(): pl.pallas_call(kernel, out_shape=(jax.ShapeDtypeStruct((N_GX, TILE, TILE)...  83.6 us
    unnamed x14, local copies, waits for them, and re-layouts  8.61 us

profile of v1, /device:TPU:43, one launch (start us, length us, event | category | flops | bytes accessed | tf_op | source)
XLA Modules:
  0.0 93.9 jit_solution(6782966799035149942)
XLA Ops:
  0.6 0.7 compare_select_fusion
  1.3 0.1 eq.15
  1.4 0.1 select_reduce_fusion
  1.5 0.1 pad_add_fusion.plan_hbm
  1.6 0.0 copy-start
  1.6 2.2 %copy-done = f32[1024,1024]{1,0:T(8,128)S(1)} copy-done((f32[1024,1024]{1,0:T(8,128)S(1)}, f32[1024,1024]{1,0:T(8,128)}, u32[]{:S(2)}) %copy-start) | copy-done | bytes 4194328
  3.8 0.0 copy-start.1
  3.8 0.9 copy-done.1
  4.7 0.0 copy-start.2
  4.7 0.8 copy-done.2
  5.6 0.0 copy-start.3
  5.6 0.7 copy-done.3
  6.2 0.0 copy-start.4
  6.2 0.7 copy-done.4
  6.9 0.0 copy-start.5
  6.9 0.7 copy-done.5
  7.5 83.6 %shard_map.104 = (f32[16,256,256]{2,1,0:T(8,128)S(1)}, f32[4,128,128]{2,1,0:T(8,128)S(1)}) custom-call(f32[1024,1024]{1,0:T(8,128)S(1)} %copy-done, s32[1024,1024]{1,0:T(8,128)} %fuel_hbm.1, s32[128,128]{1,0:T(8,128)S(1)} %copy-done.2, f32[2,128,128]{2,1,0:T(8,128)S(1)} %copy-done.1, f32[13]{0:T(128)S(1)} %copy-done.3, f32[13]{0:T(128)S(1)} %copy-done.4, ...), custom_call_target="tpu_custom_call" | custom-call | tf_op jit(solution)/shard_map/pallas_call | solution.py:457
  91.1 2.0 %copy.13 = f32[1,16,256,256]{3,2,1,0:T(8,128)} copy(f32[1,16,256,256]{3,2,1,0:T(8,128)S(1)} %bitcast.1) | data formatting | bytes 8388608
  93.2 0.7 copy.14
Async XLA Ops:
  1.6 2.2 %copy-start = (f32[1024,1024]{1,0:T(8,128)S(1)}, f32[1024,1024]{1,0:T(8,128)}, u32[]{:S(2)}) copy-start(f32[1024,1024]{1,0:T(8,128)} %level_hbm.1) | copy-start | bytes 12582916
  3.8 0.9 copy-start.1
  4.7 0.8 copy-start.2
  5.6 0.7 copy-start.3
  6.2 0.7 copy-start.4
  6.9 0.7 copy-start.5

commit v2 on v1

--- a/solution.py
+++ b/solution.py
@@ -17,6 +17,9 @@
 COARSE = 128
 RING = 384
 TINY = 1e-30
+PARTS = 4
+PART = TILE // PARTS
+GROUPS = PART // 8
 MESH = pl.DeviceIdType.MESH
 F32 = jnp.float32
 BF16 = jnp.bfloat16
@@ -75,7 +78,7 @@
 def kernel(
     level_hbm, fuel_hbm, ignition_hbm, wind_hbm, spread_hbm, heat_hbm, plan_hbm, profile_hbm,
     out, heating,
-    levels, spreads, fuels, winds, level, spread, heat, halfway, fire_wind,
+    levels, spreads, fuels, winds, halfway, fire_wind,
     ignition, wind, spread_table, heat_table, plan, profile,
     wind_pad, row_weight, ignite, stage, release, flux,
     row_send, row_recv, col_send, col_recv, diag_send, diag_recv,
@@ -345,7 +348,9 @@
     def eight(i):
         return pl.ds(pl.multiple_of(i * 8, 8), 8)
 
-    def one_tile(j, carry):
+    def one_part(n, carry):
+        c = n // len(OFFSETS)
+        j = n % len(OFFSETS)
         ox = jnp.int32(0)
         oy = jnp.int32(0)
         for i, (dx, dy) in enumerate(OFFSETS):
@@ -355,69 +360,77 @@
         target = ((my_x + ox) % 4) * 4 + (my_y + oy) % 4
 
         chosen = plan[target]
-        level[0 : TILE + 16, :] = levels[chosen]
-        spread[...] = spreads[chosen]
-        heat[...] = lookup(heat_table, 1.0 / (2.0 * TIME_STEP * REFINE * REFINE), fuels[chosen])
-        fire_wind[...] = jnp.dot(row_weight[...], winds[chosen], preferred_element_type=F32)
-
-        def first(i, carry):
-            above, centre = carry
-            below = level[eight(i + 1), :]
+        part = pl.ds(pl.multiple_of(c * PART, PART), PART)
+        fire_wind[...] = jnp.dot(
+            row_weight[pl.ds(pl.multiple_of(c * PART, PART), PART + 16), :],
+            winds[chosen],
+            preferred_element_type=F32,
+        )
+
+        def level_rows(i):
+            return levels[chosen, eight(c * GROUPS + i), :]
+
+        above = centre = level_rows(0)
+        for i in range(GROUPS + 2):
+            below = level_rows(i + 1) if i < GROUPS + 1 else centre
             up = pltpu.roll(jnp.where(sub == 7, above, centre), 1, 0)
             down = pltpu.roll(jnp.where(sub == 0, below, centre), 7, 0)
             left = pltpu.roll(centre, 1, 1)
             right = pltpu.roll(centre, RING - 1, 1)
-            halfway[eight(i), :] = advance(
+            rows = slice(i * 8, i * 8 + 8)
+            halfway[rows, :] = advance(
                 centre, up, down, left, right,
-                fire_wind[eight(i), 0:RING], fire_wind[eight(i), RING : 2 * RING],
-                spread[eight(i), :],
-            )
-            return centre, below
-
-        level[TILE + 16 :, :] = level[TILE + 8 : TILE + 16, :]
-        lax.fori_loop(0, TILE // 8 + 2, first, (level[0:8, :], level[0:8, :]), unroll=2)
-
-        def second(i, carry):
-            above, centre = carry
-            below = halfway[eight(i + 2), :]
+                fire_wind[rows, 0:RING], fire_wind[rows, RING : 2 * RING],
+                spreads[chosen, eight(c * GROUPS + i), :],
+            )
+            above, centre = centre, below
+
+        above, centre = halfway[0:8, :], halfway[8:16, :]
+        for i in range(GROUPS):
+            below = halfway[i * 8 + 16 : i * 8 + 24, :]
             inner = centre[:, 0:TILE]
             up = pltpu.roll(jnp.where(sub_in == 7, above[:, 0:TILE], inner), 1, 0)
             down = pltpu.roll(jnp.where(sub_in == 0, below[:, 0:TILE], inner), 7, 0)
             left = pltpu.roll(centre, 1, 1)[:, 0:TILE]
             right = pltpu.roll(centre, RING - 1, 1)[:, 0:TILE]
+            rows = slice(i * 8 + 8, i * 8 + 16)
+            padded = eight(c * GROUPS + i + 1)
             result = advance(
                 inner, up, down, left, right,
-                fire_wind[eight(i + 1), 0:TILE], fire_wind[eight(i + 1), RING : RING + TILE],
-                spread[eight(i + 1), 0:TILE],
-            )
-            before = jnp.clip(0.5 - level[eight(i + 1), 0:TILE], 0.0, 1.0)
+                fire_wind[rows, 0:TILE], fire_wind[rows, RING : RING + TILE],
+                spreads[chosen, padded, 0:TILE],
+            )
+            before = jnp.clip(0.5 - levels[chosen, padded, 0:TILE], 0.0, 1.0)
             after = jnp.clip(0.5 - result, 0.0, 1.0)
-            released = heat[eight(i), :] * (after - before)
-            release[0, eight(i), :] = released[:, 0:128]
-            release[1, eight(i), :] = released[:, 128:256]
-            stage[target, eight(i), :] = result
-            return centre, below
-
-        lax.fori_loop(0, TILE // 8, second, (halfway[0:8, :], halfway[8:16, :]), unroll=2)
+            heat = lookup(
+                heat_table, 1.0 / (2.0 * TIME_STEP * REFINE * REFINE), fuels[chosen, eight(c * GROUPS + i), :]
+            )
+            released = heat * (after - before)
+            release[0, i * 8 : i * 8 + 8, :] = released[:, 0:128]
+            release[1, i * 8 : i * 8 + 8, :] = released[:, 128:256]
+            stage[target, eight(c * GROUPS + i), :] = result
+            above, centre = centre, below
 
         @pl.when(j < len(OFFSETS) - 1)
         def _():
             pltpu.make_async_remote_copy(
-                src_ref=stage.at[target], dst_ref=out.at[gx],
-                send_sem=send_sem.at[j], recv_sem=recv_sem.at[j],
+                src_ref=stage.at[target, part], dst_ref=out.at[gx, part],
+                send_sem=send_sem.at[j, c], recv_sem=recv_sem.at[j, c],
                 device_id={"gx": target, "gy": gy}, device_id_type=MESH,
             ).start()
 
-        rows = []
+        sums = []
         for half in range(2):
-            total = release[half, pl.ds(0, 32, stride=8), :]
+            total = release[half, pl.ds(0, GROUPS, stride=8), :]
             for s in range(1, 8):
-                total = total + release[half, pl.ds(s, 32, stride=8), :]
-            rows.append(total)
-        flux[target] = dot2(jnp.concatenate(rows, axis=1), place)
+                total = total + release[half, pl.ds(s, GROUPS, stride=8), :]
+            sums.append(total)
+        flux[target, pl.ds(pl.multiple_of(c * GROUPS, GROUPS), GROUPS), :] = dot2(
+            jnp.concatenate(sums, axis=1), place
+        )
         return carry
 
-    lax.fori_loop(0, len(OFFSETS), one_tile, 0)
+    lax.fori_loop(0, PARTS * len(OFFSETS), one_part, 0)
 
     own = pltpu.make_async_copy(stage.at[gx], out.at[gx], own_sem)
     own.start()
@@ -432,11 +445,13 @@
     own.wait()
 
     def finish(j, carry):
-        pltpu.make_async_remote_copy(
-            src_ref=stage.at[gx], dst_ref=out.at[gx],
-            send_sem=send_sem.at[j], recv_sem=recv_sem.at[j],
-            device_id={"gx": (gx + 1) % N_GX, "gy": gy}, device_id_type=MESH,
-        ).wait()
+        for c in range(PARTS):
+            part = pl.ds(c * PART, PART)
+            pltpu.make_async_remote_copy(
+                src_ref=stage.at[gx, part], dst_ref=out.at[gx, part],
+                send_sem=send_sem.at[j, c], recv_sem=recv_sem.at[j, c],
+                device_id={"gx": (gx + 1) % N_GX, "gy": gy}, device_id_type=MESH,
+            ).wait()
         return carry
 
     lax.fori_loop(0, len(OFFSETS) - 1, finish, 0)
@@ -467,11 +482,8 @@
             pltpu.VMEM((17, TILE + 16, RING), F32),
             pltpu.VMEM((17, TILE, TILE), jnp.int32),
             pltpu.VMEM((17, 96, 2 * RING), BF16),
-            pltpu.VMEM((TILE + 24, RING), F32),
-            pltpu.VMEM((TILE + 16, RING), F32),
-            pltpu.VMEM((TILE, TILE), F32),
-            pltpu.VMEM((TILE + 16, RING), F32),
-            pltpu.VMEM((TILE + 16, 2 * RING), F32),
+            pltpu.VMEM((PART + 16, RING), F32),
+            pltpu.VMEM((PART + 16, 2 * RING), F32),
             pltpu.VMEM((COARSE, COARSE), jnp.int32),
             pltpu.VMEM((2, COARSE, COARSE), F32),
             pltpu.SMEM((NFUEL,), F32),
@@ -482,7 +494,7 @@
             pltpu.VMEM((TILE + 16, 96), BF16),
             pltpu.VMEM((4, COARSE, TILE), F32),
             pltpu.VMEM((N_GX, TILE, TILE), F32),
-            pltpu.VMEM((2, TILE, 128), F32),
+            pltpu.VMEM((2, PART, 128), F32),
             pltpu.VMEM((17, 32, 128), F32),
             pltpu.VMEM((2, 16, SIDE + 128), F32),
             pltpu.VMEM((2, 16, SIDE + 128), F32),
@@ -499,12 +511,12 @@
             dma((2,)),
             dma((2,)),
             dma((4,)),
-            dma((16,)),
-            dma((16,)),
+            dma((16, PARTS)),
+            dma((16, PARTS)),
             dma,
         ],
         compiler_params=pltpu.CompilerParams(
-            collective_id=0, has_side_effects=True, vmem_limit_bytes=44 << 20
+            collective_id=0, has_side_effects=True, vmem_limit_bytes=49 << 20
         ),
     )(
         level_set, fuel_class, ignition, surface_wind, spread_table, heat_table, plan, profile

time: 94.2 us -> 78.1 us (0.83)
  the two profiles are of different devices: /device:TPU:43 before, /device:TPU:37 now
where the time goes in v2:
time: 78.1 us; the launch traced here: 77.5 us
  Pallas kernels  69.5 us (89%)
  local copies, waits for them, and re-layouts  6.51 us (8%)
  other arithmetic  0.9 us (1%)
    pallas_call x1, Pallas kernels, body(): pl.pallas_call(kernel, out_shape=(jax.ShapeDtypeStruct((N_GX, TILE, TILE)...  69.5 us
    unnamed x12, local copies, waits for them, and re-layouts  6.43 us

profile of v2, /device:TPU:37, one launch (start us, length us, event | category | flops | bytes accessed | tf_op | source)
XLA Modules:
  0.0 77.5 jit_solution(11139192990766769590)
XLA Ops:
  0.6 0.7 compare_select_fusion
  1.3 0.1 eq.15
  1.4 0.1 select_reduce_fusion
  1.5 0.1 pad_add_fusion.plan_hbm
  1.6 0.0 copy-start
  1.6 0.9 %copy-done = f32[2,128,128]{2,1,0:T(8,128)S(1)} copy-done((f32[2,128,128]{2,1,0:T(8,128)S(1)}, f32[2,128,128]{2,1,0:T(8,128)}, u32[]{:S(2)}) %copy-start) | copy-done | bytes 131096
  2.5 0.0 copy-start.1
  2.5 0.8 %copy-done.1 = s32[128,128]{1,0:T(8,128)S(1)} copy-done((s32[128,128]{1,0:T(8,128)S(1)}, s32[128,128]{1,0:T(8,128)}, u32[]{:S(2)}) %copy-start.1) | copy-done | bytes 65560
  3.4 0.0 copy-start.2
  3.4 0.7 copy-done.2
  4.0 0.0 copy-start.3
  4.0 0.7 copy-done.3
  4.7 0.0 copy-start.4
  4.7 0.7 copy-done.4
  5.3 69.5 %shard_map.104 = (f32[16,256,256]{2,1,0:T(8,128)S(1)}, f32[4,128,128]{2,1,0:T(8,128)S(1)}) custom-call(f32[1024,1024]{1,0:T(8,128)} %level_hbm.1, s32[1024,1024]{1,0:T(8,128)} %fuel_hbm.1, s32[128,128]{1,0:T(8,128)S(1)} %copy-done.1, f32[2,128,128]{2,1,0:T(8,128)S(1)} %copy-done, f32[13]{0:T(128)S(1)} %copy-done.2, f32[13]{0:T(128)S(1)} %copy-done.3, ...), custom_call_target="tpu_custom_call" | custom-call | tf_op jit(solution)/shard_map/pallas_call | solution.py:472
  74.8 2.0 %copy.13 = f32[1,16,256,256]{3,2,1,0:T(8,128)} copy(f32[1,16,256,256]{3,2,1,0:T(8,128)S(1)} %bitcast.1) | data formatting | bytes 8388608
  76.8 0.7 copy.14
Async XLA Ops:
  1.6 0.9 %copy-start = (f32[2,128,128]{2,1,0:T(8,128)S(1)}, f32[2,128,128]{2,1,0:T(8,128)}, u32[]{:S(2)}) copy-start(f32[2,128,128]{2,1,0:T(8,128)} %wind_hbm.1) | copy-start | bytes 393220
  2.5 0.8 %copy-start.1 = (s32[128,128]{1,0:T(8,128)S(1)}, s32[128,128]{1,0:T(8,128)}, u32[]{:S(2)}) copy-start(s32[128,128]{1,0:T(8,128)} %ignition_hbm.1) | copy-start | bytes 196612
  3.4 0.7 copy-start.2
  4.0 0.7 copy-start.3
  4.7 0.7 copy-start.4

commit v3 on v2

--- a/solution.py
+++ b/solution.py
@@ -24,10 +24,7 @@
 F32 = jnp.float32
 BF16 = jnp.bfloat16
 
-OFFSETS = (
-    (2, 2), (2, 1), (1, 2), (2, 3), (3, 2), (1, 1), (3, 3), (1, 3),
-    (3, 1), (2, 0), (0, 2), (1, 0), (0, 1), (3, 0), (0, 3), (0, 0),
-)
+OFFSETS = ((2, 2), (0, 1), (1, 0), (0, 3), (3, 0), (2, 1), (1, 2), (2, 3), (3, 2), (0, 2), (2, 0), (1, 1), (3, 3), (1, 3), (3, 1), (0, 0))
 
 
 def split(x):
@@ -469,6 +466,10 @@
     taken = jnp.min(jnp.where(target[None, :] == ids[:, None], ids[None, :], 16), axis=1)
     plan = jnp.concatenate([taken, target])
 
+    ignition, surface_wind, spread_table, heat_table, profile = (
+        pltpu.with_memory_space_constraint(x, pltpu.HBM)
+        for x in (ignition, surface_wind, spread_table, heat_table, profile)
+    )
     relocated, heating = pl.pallas_call(
         kernel,
         out_shape=(

time: 78.1 us -> 71.7 us (0.918)
  local copies, waits for them, and re-layouts: 6.51 us -> 2.8 us
  Pallas kernels: 69.5 us -> 67.3 us
    unnamed x12 -> x2, local copies, waits for them, and re-layouts: 6.43 us -> 2.72 us
    pallas_call x1, Pallas kernels: 69.5 us -> 67.3 us  [body(): pl.pallas_call(kernel, out_shape=(jax.ShapeDtypeStruct((N_GX, TILE, TILE)...]
where the time goes in v3:
time: 71.7 us; the launch traced here: 71.6 us
  Pallas kernels  67.3 us (94%)
  local copies, waits for them, and re-layouts  2.8 us (4%)
  other arithmetic  0.9 us (1%)
    pallas_call x1, Pallas kernels, body(): pl.pallas_call(kernel, out_shape=(jax.ShapeDtypeStruct((N_GX, TILE, TILE)...  67.3 us
    unnamed x2, local copies, waits for them, and re-layouts  2.72 us

profile of v3, /device:TPU:37, one launch (start us, length us, event | category | flops | bytes accessed | tf_op | source)
XLA Modules:
  0.0 71.6 jit_solution(6929321055032815785)
XLA Ops:
  0.6 0.7 compare_select_fusion
  1.3 0.1 eq.15
  1.4 0.1 select_reduce_fusion
  1.5 0.1 pad_add_fusion.plan_hbm
  1.6 67.3 %shard_map.104 = (f32[16,256,256]{2,1,0:T(8,128)S(1)}, f32[4,128,128]{2,1,0:T(8,128)S(1)}) custom-call(f32[1024,1024]{1,0:T(8,128)} %level_hbm.1, s32[1024,1024]{1,0:T(8,128)} %fuel_hbm.1, s32[128,128]{1,0:T(8,128)} %ignition_hbm.1, f32[2,128,128]{2,1,0:T(8,128)} %wind_hbm.1, f32[13]{0:T(128)} %spread_hbm.1, f32[13]{0:T(128)} %heat_hbm.1, ...), custom_call_target="tpu_custom_call" | custom-call | tf_op jit(solution)/shard_map/pallas_call | solution.py:473
  68.9 2.0 %copy.13 = f32[1,16,256,256]{3,2,1,0:T(8,128)} copy(f32[1,16,256,256]{3,2,1,0:T(8,128)S(1)} %bitcast.1) | data formatting | bytes 8388608
  70.9 0.7 copy.14

commit v4 on v3

--- a/solution.py
+++ b/solution.py
@@ -20,6 +20,7 @@
 PARTS = 4
 PART = TILE // PARTS
 GROUPS = PART // 8
+EDGE_FIRST = (0, 3, 4, 7, 8, 11, 12, 15, 1, 2, 13, 14, 5, 6, 9, 10)
 MESH = pl.DeviceIdType.MESH
 F32 = jnp.float32
 BF16 = jnp.bfloat16
@@ -73,10 +74,10 @@
 
 
 def kernel(
-    level_hbm, fuel_hbm, ignition_hbm, wind_hbm, spread_hbm, heat_hbm, plan_hbm, profile_hbm,
+    level_hbm, fuel_hbm, ignition_hbm, wind_hbm, spread_hbm, heat_hbm, destination_hbm, profile_hbm,
     out, heating,
     levels, spreads, fuels, winds, halfway, fire_wind,
-    ignition, wind, spread_table, heat_table, plan, profile,
+    ignition, wind, spread_table, heat_table, destination, profile, plan,
     wind_pad, row_weight, ignite, stage, release, flux,
     row_send, row_recv, col_send, col_recv, diag_send, diag_recv,
     small_sem, level_sem, fuel_sem,
@@ -93,13 +94,13 @@
         pltpu.make_async_copy(source, here, small_sem.at[n])
         for n, (source, here) in enumerate((
             (ignition_hbm, ignition), (spread_hbm, spread_table), (wind_hbm, wind),
-            (heat_hbm, heat_table), (plan_hbm, plan), (profile_hbm, profile),
+            (heat_hbm, heat_table), (destination_hbm, destination), (profile_hbm, profile),
         ))
     ]
     for copy in small:
         copy.start()
     loads = []
-    for k in range(16):
+    for k in EDGE_FIRST:
         block = (pl.ds(k // 4 * TILE, TILE), pl.ds(k % 4 * TILE, TILE))
         loads.append(
             pltpu.make_async_copy(
@@ -139,6 +140,14 @@
 
     for copy in small:
         copy.wait()
+    goes = [destination[k // 4, k % 4] for k in range(16)]
+    for k in range(16):
+        plan[16 + k] = goes[k] + 17 * (goes[k] < 0).astype(jnp.int32)
+    for d in range(16):
+        taken = jnp.int32(16)
+        for k in range(16):
+            taken = taken + (goes[k] == d).astype(jnp.int32) * (k - taken)
+        plan[d] = taken
     cell = lax.broadcasted_iota(jnp.int32, (COARSE, TILE), 0)
     at = lax.broadcasted_iota(jnp.int32, (COARSE, TILE), 1) // REFINE
     burning = ignition[...].astype(F32).astype(BF16)
@@ -157,7 +166,7 @@
                 codes = fuels[k, pl.ds(pl.multiple_of(block * 64 + s * 8, 8), 8), lanes]
                 spreads[k, inner, lanes] = lookup(spread_table, TIME_STEP, codes)
 
-    for copy in loads:
+    for copy in loads[:24]:
         copy.wait()
 
     def prepare_edges(block, carry):
@@ -236,6 +245,9 @@
     for copy in halos:
         copy.start()
 
+    for copy in loads[24:]:
+        copy.wait()
+
     def prepare_rest(block, carry):
         for tile_y, halves in ((0, (1,)), (1, (0, 1)), (2, (0, 1)), (3, (0,))):
             prepare(block // 4, tile_y, block % 4, range(8), halves)
@@ -461,14 +473,9 @@
     vmem = pl.BlockSpec(memory_space=pltpu.VMEM)
     dma = pltpu.SemaphoreType.DMA
 
-    target = jnp.where(counts > 0, destination, 16).reshape(16)
-    ids = jnp.arange(16, dtype=jnp.int32)
-    taken = jnp.min(jnp.where(target[None, :] == ids[:, None], ids[None, :], 16), axis=1)
-    plan = jnp.concatenate([taken, target])
-
-    ignition, surface_wind, spread_table, heat_table, profile = (
+    ignition, surface_wind, spread_table, heat_table, destination, profile = (
         pltpu.with_memory_space_constraint(x, pltpu.HBM)
-        for x in (ignition, surface_wind, spread_table, heat_table, profile)
+        for x in (ignition, surface_wind, spread_table, heat_table, destination, profile)
     )
     relocated, heating = pl.pallas_call(
         kernel,
@@ -489,8 +496,9 @@
             pltpu.VMEM((2, COARSE, COARSE), F32),
             pltpu.SMEM((NFUEL,), F32),
             pltpu.SMEM((NFUEL,), F32),
+            pltpu.SMEM((4, 4), jnp.int32),
+            pltpu.SMEM((LEV,), F32),
             pltpu.SMEM((32,), jnp.int32),
-            pltpu.SMEM((LEV,), F32),
             pltpu.VMEM((2, COARSE + 16, 256), F32),
             pltpu.VMEM((TILE + 16, 96), BF16),
             pltpu.VMEM((4, COARSE, TILE), F32),
@@ -520,7 +528,7 @@
             collective_id=0, has_side_effects=True, vmem_limit_bytes=49 << 20
         ),
     )(
-        level_set, fuel_class, ignition, surface_wind, spread_table, heat_table, plan, profile
+        level_set, fuel_class, ignition, surface_wind, spread_table, heat_table, destination, profile
     )
     return relocated.reshape(1, N_GX, TILE, TILE), heating
 

time: 71.7 us -> 71 us (level)
  other arithmetic: 0.9 us -> 0 us
where the time goes in v4:
time: 71 us; the launch traced here: 70.9 us
  Pallas kernels  67.6 us (95%)
  local copies, waits for them, and re-layouts  2.72 us (4%)
    pallas_call x1, Pallas kernels, body(): pl.pallas_call(kernel, out_shape=(jax.ShapeDtypeStruct((N_GX, TILE, TILE)...  67.6 us
    unnamed x2, local copies, waits for them, and re-layouts  2.72 us

profile of v4, /device:TPU:37, one launch (start us, length us, event | category | flops | bytes accessed | tf_op | source)
XLA Modules:
  0.0 70.9 jit_solution(9741653283241686663)
XLA Ops:
  0.6 67.6 %shard_map.95 = (f32[16,256,256]{2,1,0:T(8,128)S(1)}, f32[4,128,128]{2,1,0:T(8,128)S(1)}) custom-call(f32[1024,1024]{1,0:T(8,128)} %level_hbm.1, s32[1024,1024]{1,0:T(8,128)} %fuel_hbm.1, s32[128,128]{1,0:T(8,128)} %ignition_hbm.1, f32[2,128,128]{2,1,0:T(8,128)} %wind_hbm.1, f32[13]{0:T(128)} %spread_hbm.1, f32[13]{0:T(128)} %heat_hbm.1, ...), custom_call_target="tpu_custom_call" | custom-call | tf_op jit(solution)/shard_map/pallas_call | solution.py:480
  68.2 2.0 %copy.12 = f32[1,16,256,256]{3,2,1,0:T(8,128)} copy(f32[1,16,256,256]{3,2,1,0:T(8,128)S(1)} %bitcast.1) | data formatting | bytes 8388608
  70.2 0.7 copy.13
